TPU v7x, 512 devices: a whole 4x4x16 slice. The times are simulated.
512 devices in a mesh: site: 16 (over z), bond: 32 (over y, x, core).
Axes of the slice: x: 4, y: 4, z: 16, core: 2. Of those that a mesh axis runs over, the one named last changes fastest.
Arguments:
- site_tensor: float32 [16, 4, 3072, 3072], P('site', None, 'bond'), may hold values from -0.21875 to 0.21875
- panels: float32 [16, 3072, 128], P('site', 'bond'), may hold values from -6 to 6
- fresh: float32 [1, 3072, 128], P(None, 'bond'), may hold values from -6 to 6
- outcomes: int32 [16, 2, 128], P('site'), may hold values from 0 to 3, as said below
Outputs:
- carried: float32 [16, 2, 3072, 128], P('site', None, 'bond')
Inputs may be any that keep to these rules, and one draw needn't show every extreme that they name: `outcomes`: at each site and tick, every outcome is taken by at most 48 samples, and some outcome by exactly 48.
All inputs are finite; a program needn't handle non-finite values.
Results may differ from a plain program's by a relative error of at most 0.0001.
Values sent between devices are 32-bit elements; how exact they have to be, the bound alone decides.
No kernel may reach another device: no remote copies, remote signals or barrier semaphores. Data moves between devices by JAX's collectives and lax.ppermute only.
A program may use at most 64 MiB of HBM per device.

v0:
```python
import jax
import jax.numpy as jnp
from jax import lax
from jax.sharding import PartitionSpec as P

TICKS = 2


def from_behind(value, axis, steps):
    count = lax.axis_size(axis)
    initial, last = (max(0, -steps), min(count, count - steps))
    return lax.ppermute(value, axis, [(source, source + steps) for source in range(initial, last)])


def contribute(tensor, vectors, selected):
    outcome_count = tensor.shape[0]
    chosen = (selected[None, :] == jnp.arange(outcome_count, dtype=jnp.int32)[:, None]).astype(
        jnp.float32
    )
    products = lax.dot_general(
        tensor,
        vectors,
        (((1,), (0,)), ((), ())),
        precision=lax.Precision.HIGHEST,
        preferred_element_type=jnp.float32,
    )
    return jnp.sum(products * chosen[:, None, :], axis=0)


def advance(tensor, vectors, selected):
    rows_local = tensor.shape[1]
    complete = contribute(tensor, vectors, selected)
    summed = lax.psum(complete, "bond")
    bond_index = lax.axis_index("bond")
    return lax.dynamic_slice_in_dim(summed, bond_index * rows_local, rows_local, 0)


def on_device(site_tensor, panels, fresh, outcomes):
    tensor = site_tensor[0]
    current = panels[0]
    results = []
    for tick_index in range(TICKS):
        produced = advance(tensor, current, outcomes[0, tick_index])
        results.append(produced)
        if tick_index + 1 < TICKS:
            passed = from_behind(produced, "site", 1)
            current = jnp.where(lax.axis_index("site") == 0, fresh[tick_index], passed)
    return jnp.stack(results, 0)[None]


def solution(mesh):
    placed = (
        P("site", None, "bond", None),
        P("site", "bond", None),
        P(None, "bond", None),
        P("site", None, None),
    )
    return jax.shard_map(
        on_device,
        mesh=mesh,
        in_specs=placed,
        out_specs=P("site", None, "bond", None),
        check_vma=False,
    )
```

profile of v0, /device:TPU:6, one launch (start us, length us, event | category | flops | bytes accessed | tf_op | source)
XLA Modules:
  0.0 324.4 jit_solution(2614767855735934217)
XLA Ops:
  6.5 0.0 copy-start
  6.5 0.0 copy-start.1
  6.5 0.0 all-reduce.3.cloned.1.call-start
  6.5 0.8 slice_bitcast_fusion.1
  7.3 0.1 copy-done
  7.4 13.1 %multiply_reduce_fusion = f32[3072,128]{1,0:T(8,128)} fusion(f32[1,4,96,3072]{3,2,1,0:T(8,128)} %param.4, f32[4,128]{1,0:T(4,128)S(1)} %fusion.6, f32[1,96,128]{2,1,0:T(8,128)S(1)} %copy-done), kind=kOutput, calls=%fused_computation.2 | convolution fusion | flops 1814691840 | bytes 6342656 | tf_op jit(solution)/shard_map/dot_general | solution.py:20
  20.4 0.0 all-reduce.3.cloned.1.call-update
  20.4 0.0 all-reduce.5.cloned.1.call-start
  20.5 142.2 %all-reduce.3.cloned.1.call-done = f32[3072,128]{1,0:T(8,128)} async-done(((f32[3072,128]{1,0:T(8,128)}), f32[3072,128]{1,0:T(8,128)}) %all-reduce.3.cloned.1.call-update) | async-done | bytes 1572880 | tf_op jit(solution)/shard_map/psum | solution.py:33
  162.7 0.8 constant_dynamic-slice_fusion.1
  163.5 3.4 %collective-permute-start = (f32[96,128]{1,0:T(8,128)S(1)}, f32[96,128]{1,0:T(8,128)S(1)}, u32[]{:S(2)}, u32[]{:S(2)}) collective-permute-start(f32[96,128]{1,0:T(8,128)S(1)} %constant_dynamic-slice_fusion.1), channel_id=1, source_target_pairs={{0,32},{32,64},{64,96},{96,128},{128,160},{160,192},{192,224},{224... | collective-permute-start | bytes 147464 | tf_op jit(solution)/shard_map/ppermute | solution.py:12
  167.0 1.7 collective-permute-done
  168.7 0.0 copy-done.1
  168.7 8.6 %fusion = f32[3072,128]{0,1:T(8,128)} fusion(f32[1,4,96,3072]{3,2,1,0:T(8,128)} %param.4, f32[4,128]{1,0:T(4,128)S(1)} %fusion.7, f32[96,128]{1,0:T(8,128)S(1)} %collective-permute-done, f32[1,96,128]{2,1,0:T(8,128)S(1)} %copy-done.1, pred[]{:T(512)S(6)} %eq.45), kind=kOutput, calls=%fused_computation.1 | convolution fusion | flops 1814704128 | bytes 6391809 | tf_op jit(solution)/shard_map/dot_general | solution.py:20
  177.3 0.0 all-reduce.5.cloned.1.call-update
  177.4 0.8 fusion.8
  178.2 137.6 %all-reduce.5.cloned.1.call-done = f32[3072,128]{0,1:T(8,128)} async-done(((f32[3072,128]{0,1:T(8,128)}), f32[3072,128]{0,1:T(8,128)}) %all-reduce.5.cloned.1.call-update) | async-done | bytes 1572880 | tf_op jit(solution)/shard_map/psum | solution.py:33
  315.8 1.0 constant_dynamic-slice_fusion
  316.8 0.1 copy.5
  316.9 0.7 maximum_bitcast_fusion
  (2 shorter events, 0.0 us)
Async XLA Ops:
  6.5 0.8 copy-start
  6.5 162.2 %copy-start.1 = (f32[1,96,128]{2,1,0:T(8,128)S(1)}, f32[1,96,128]{2,1,0:T(8,128)}, u32[]{:S(2)}) copy-start(f32[1,96,128]{2,1,0:T(8,128)} %param.6) | copy-start | bytes 147460
  6.5 156.2 %all-reduce.3.cloned.1.call-start = ((), (), s32[]{:S(2)}) async-start(), calls=%async_computation | async-start | bytes 3145728 | tf_op jit(solution)/shard_map/psum | solution.py:33
  20.4 295.4 %all-reduce.5.cloned.1.call-start = ((), (), s32[]{:S(2)}) async-start(), calls=%async_computation.1 | async-start | bytes 3145728 | tf_op jit(solution)/shard_map/psum | solution.py:33
  163.5 5.2 %collective-permute-start = (f32[96,128]{1,0:T(8,128)S(1)}, f32[96,128]{1,0:T(8,128)S(1)}, u32[]{:S(2)}, u32[]{:S(2)}) collective-permute-start(f32[96,128]{1,0:T(8,128)S(1)} %constant_dynamic-slice_fusion.1), channel_id=1, source_target_pairs={{0,32},{32,64},{64,96},{96,128},{128,160},{160,192},{192,224},{224... | collective-permute-start | bytes 147464 | tf_op jit(solution)/shard_map/ppermute | solution.py:12
Sparse Core Ops, SparseCore 0:
  20.6 142.1 all-reduce.2
  177.5 138.2 all-reduce.4
where the time goes:
time: 325 us; the launch traced here: 324 us
  waiting for transfers between devices  282 us (87%)
  matrix products  21.7 us (7%)
  between operations  13.4 us (4%)
  local copies, waits for them, and re-layouts  3.5 us (1%)
  starting transfers between devices  3.49 us (1%)
    psum x2, waiting for transfers between devices, advance(): summed = lax.psum(complete, 'bond')  280 us
    dot_general x2, matrix products, contribute(): lax.dot_general(tensor, vectors, (((1,), (0,)), ((), ())), precision=lax....  21.7 us
  transfers between devices with their start and end apart: 3, of which 3 were waited for; matrix products, arithmetic and copies ran while one was open for 0% of the time, Pallas kernels for 0%

commit v1 on v0

--- a/solution.py
+++ b/solution.py
@@ -30,7 +30,9 @@
 def advance(tensor, vectors, selected):
     rows_local = tensor.shape[1]
     complete = contribute(tensor, vectors, selected)
-    summed = lax.psum(complete, "bond")
+    summed = complete
+    for hop in (1, 2, 4, 8, 16):
+        summed = summed + lax.ppermute(summed, "bond", [(dev, dev ^ hop) for dev in range(32)])
     bond_index = lax.axis_index("bond")
     return lax.dynamic_slice_in_dim(summed, bond_index * rows_local, rows_local, 0)
 

time: 325 us -> 345 us (1.062)
  starting transfers between devices: 3.49 us -> 31.9 us
  between operations: 13.4 us -> 0.19 us
  waiting for transfers between devices: 282 us -> 288 us
    ppermute x0 -> x10, waiting for transfers between devices: none -> 286 us  [advance(): lax.ppermute(summed, 'bond', [(dev, dev ^ hop) for dev in range(32)])]
    psum x2 -> x0, waiting for transfers between devices: 280 us -> none  [advance(): summed = lax.psum(complete, 'bond')]
    ppermute x0 -> x10, starting transfers between devices: none -> 30.7 us  [advance(): lax.ppermute(summed, 'bond', [(dev, dev ^ hop) for dev in range(32)])]
  transfers between devices with their start and end apart: 3 -> 11, of which waited for: 3 -> 11; matrix products, arithmetic and copies ran while one was open for 0% -> 0% of each run, Pallas kernels for 0% -> 0%
where the time goes in v1:
time: 345 us; the launch traced here: 343 us
  waiting for transfers between devices  288 us (83%)
  starting transfers between devices  31.9 us (9%)
  matrix products  19.5 us (6%)
    ppermute x10, waiting for transfers between devices, advance(): lax.ppermute(summed, 'bond', [(dev, dev ^ hop) for dev in range(32)])  286 us
    ppermute x10, starting transfers between devices, advance(): lax.ppermute(summed, 'bond', [(dev, dev ^ hop) for dev in range(32)])  30.7 us
    dot_general x2, matrix products, contribute(): lax.dot_general(tensor, vectors, (((1,), (0,)), ((), ())), precision=lax....  19.5 us
  transfers between devices with their start and end apart: 11, of which 11 were waited for; matrix products, arithmetic and copies ran while one was open for 0% of the time, Pallas kernels for 0%

profile of v1, /device:TPU:6, one launch (start us, length us, event | category | flops | bytes accessed | tf_op | source)
XLA Modules:
  0.0 342.6 jit_solution(9482945624864605307)
XLA Ops:
  0.0 0.0 copy-start
  0.0 0.8 slice_bitcast_fusion.1
  0.8 0.1 copy-done
  0.8 11.9 %multiply_reduce_fusion = f32[3072,128]{1,0:T(8,128)S(1)} fusion(f32[1,4,96,3072]{3,2,1,0:T(8,128)} %param.4, f32[4,128]{1,0:T(4,128)S(1)} %fusion.6, f32[1,96,128]{2,1,0:T(8,128)S(1)} %copy-done), kind=kOutput, calls=%fused_computation.2 | convolution fusion | flops 1814691840 | bytes 6342656 | tf_op jit(solution)/shard_map/dot_general | solution.py:20
  12.8 1.9 collective-permute-start
  14.7 3.4 collective-permute-done
  18.1 0.2 add.34
  18.3 2.7 collective-permute-start.1
  21.0 35.6 %collective-permute-done.1 = f32[3072,128]{1,0:T(8,128)S(1)} collective-permute-done((f32[3072,128]{1,0:T(8,128)S(1)}, f32[3072,128]{1,0:T(8,128)S(1)}, u32[]{:S(2)}, u32[]{:S(2)}) %collective-permute-start.1) | collective-permute-done | bytes 1572896 | tf_op jit(solution)/shard_map/ppermute | solution.py:35
  56.6 0.2 add.35
  56.8 7.5 %collective-permute-start.2 = (f32[3072,128]{1,0:T(8,128)S(1)}, f32[3072,128]{1,0:T(8,128)S(1)}, u32[]{:S(2)}, u32[]{:S(2)}) collective-permute-start(f32[3072,128]{1,0:T(8,128)S(1)} %add.35), channel_id=1, source_target_pairs={{0,4},{1,5},{2,6},{3,7},{4,0},{5,1},{6,2},{7,3},{8,12},{9,13},{10,... | collective-permute-start | bytes 4718600 | tf_op jit(solution)/shard_map/ppermute | solution.py:35
  64.3 34.2 %collective-permute-done.2 = f32[3072,128]{1,0:T(8,128)S(1)} collective-permute-done((f32[3072,128]{1,0:T(8,128)S(1)}, f32[3072,128]{1,0:T(8,128)S(1)}, u32[]{:S(2)}, u32[]{:S(2)}) %collective-permute-start.2) | collective-permute-done | bytes 1572896 | tf_op jit(solution)/shard_map/ppermute | solution.py:35
  98.4 0.2 add.36
  98.6 0.0 copy-start.1
  98.6 2.1 collective-permute-start.3
  100.7 35.3 %collective-permute-done.3 = f32[3072,128]{1,0:T(8,128)S(1)} collective-permute-done((f32[3072,128]{1,0:T(8,128)S(1)}, f32[3072,128]{1,0:T(8,128)S(1)}, u32[]{:S(2)}, u32[]{:S(2)}) %collective-permute-start.3) | collective-permute-done | bytes 1572896 | tf_op jit(solution)/shard_map/ppermute | solution.py:35
  136.0 0.2 add.37
  136.2 1.9 collective-permute-start.4
  138.1 35.9 %collective-permute-done.4 = f32[3072,128]{1,0:T(8,128)S(1)} collective-permute-done((f32[3072,128]{1,0:T(8,128)S(1)}, f32[3072,128]{1,0:T(8,128)S(1)}, u32[]{:S(2)}, u32[]{:S(2)}) %collective-permute-start.4) | collective-permute-done | bytes 1572896 | tf_op jit(solution)/shard_map/ppermute | solution.py:35
  174.0 1.3 collective-permute-start.5
  175.3 1.7 collective-permute-done.5
  177.0 0.0 copy-done.1
  177.0 7.6 %fusion = f32[3072,128]{0,1:T(8,128)S(1)} fusion(f32[1,4,96,3072]{3,2,1,0:T(8,128)} %param.4, f32[4,128]{1,0:T(4,128)S(1)} %fusion.7, f32[96,128]{1,0:T(8,128)S(1)} %collective-permute-done.5, f32[1,96,128]{2,1,0:T(8,128)S(1)} %copy-done.1, pred[]{:T(512)S(6)} %eq.45), kind=kOutput, calls=%fused_computation.1 | convolution fusion | flops 1814704128 | bytes 6391809 | tf_op jit(solution)/shard_map/dot_general | solution.py:20
  184.6 1.9 collective-permute-start.6
  186.5 3.4 collective-permute-done.6
  189.9 0.2 add.40
  190.1 2.0 collective-permute-start.7
  192.1 36.3 %collective-permute-done.7 = f32[3072,128]{0,1:T(8,128)S(1)} collective-permute-done((f32[3072,128]{0,1:T(8,128)S(1)}, f32[3072,128]{0,1:T(8,128)S(1)}, u32[]{:S(2)}, u32[]{:S(2)}) %collective-permute-start.7) | collective-permute-done | bytes 1572896 | tf_op jit(solution)/shard_map/ppermute | solution.py:35
  228.4 0.2 add.41
  228.6 4.5 %collective-permute-start.8 = (f32[3072,128]{0,1:T(8,128)S(1)}, f32[3072,128]{0,1:T(8,128)S(1)}, u32[]{:S(2)}, u32[]{:S(2)}) collective-permute-start(f32[3072,128]{0,1:T(8,128)S(1)} %add.41), channel_id=1, source_target_pairs={{0,4},{1,5},{2,6},{3,7},{4,0},{5,1},{6,2},{7,3},{8,12},{9,13},{10,... | collective-permute-start | bytes 4718600 | tf_op jit(solution)/shard_map/ppermute | solution.py:35
  233.1 34.5 %collective-permute-done.8 = f32[3072,128]{0,1:T(8,128)S(1)} collective-permute-done((f32[3072,128]{0,1:T(8,128)S(1)}, f32[3072,128]{0,1:T(8,128)S(1)}, u32[]{:S(2)}, u32[]{:S(2)}) %collective-permute-start.8) | collective-permute-done | bytes 1572896 | tf_op jit(solution)/shard_map/ppermute | solution.py:35
  267.6 0.2 add.42
  267.8 2.5 collective-permute-start.9
  270.3 34.1 %collective-permute-done.9 = f32[3072,128]{0,1:T(8,128)S(1)} collective-permute-done((f32[3072,128]{0,1:T(8,128)S(1)}, f32[3072,128]{0,1:T(8,128)S(1)}, u32[]{:S(2)}, u32[]{:S(2)}) %collective-permute-start.9) | collective-permute-done | bytes 1572896 | tf_op jit(solution)/shard_map/ppermute | solution.py:35
  304.4 0.2 add.43
  304.6 3.7 %collective-permute-start.10 = (f32[3072,128]{0,1:T(8,128)S(1)}, f32[3072,128]{0,1:T(8,128)S(1)}, u32[]{:S(2)}, u32[]{:S(2)}) collective-permute-start(f32[3072,128]{0,1:T(8,128)S(1)} %add.43), channel_id=1, source_target_pairs={{0,16},{1,17},{2,18},{3,19},{4,20},{5,21},{6,22},{7,23},{8,24},{9,... | collective-permute-start | bytes 4718600 | tf_op jit(solution)/shard_map/ppermute | solution.py:35
  308.3 33.5 %collective-permute-done.10 = f32[3072,128]{0,1:T(8,128)S(1)} collective-permute-done((f32[3072,128]{0,1:T(8,128)S(1)}, f32[3072,128]{0,1:T(8,128)S(1)}, u32[]{:S(2)}, u32[]{:S(2)}) %collective-permute-start.10) | collective-permute-done | bytes 1572896 | tf_op jit(solution)/shard_map/ppermute | solution.py:35
  341.8 0.1 dynamic-slice_add_fusion
  341.9 0.1 copy.5
  342.0 0.7 maximum_bitcast_fusion
  (3 shorter events, 0.0 us)
Async XLA Ops:
  0.0 0.8 copy-start
  12.8 5.3 %collective-permute-start = (f32[3072,128]{1,0:T(8,128)S(1)}, f32[3072,128]{1,0:T(8,128)S(1)}, u32[]{:S(2)}, u32[]{:S(2)}) collective-permute-start(f32[3072,128]{1,0:T(8,128)S(1)} %multiply_reduce_fusion), channel_id=1, source_target_pairs={{0,1},{1,0},{2,3},{3,2},{4,5},{5,4},{6,7},{7,6},{8,9},{9,8},{10,11... | collective-permute-start | bytes 4718600 | tf_op jit(solution)/shard_map/ppermute | solution.py:35
  18.3 38.3 %collective-permute-start.1 = (f32[3072,128]{1,0:T(8,128)S(1)}, f32[3072,128]{1,0:T(8,128)S(1)}, u32[]{:S(2)}, u32[]{:S(2)}) collective-permute-start(f32[3072,128]{1,0:T(8,128)S(1)} %add.34), channel_id=1, source_target_pairs={{0,2},{1,3},{2,0},{3,1},{4,6},{5,7},{6,4},{7,5},{8,10},{9,11},{10,... | collective-permute-start | bytes 4718600 | tf_op jit(solution)/shard_map/ppermute | solution.py:35
  56.8 41.7 %collective-permute-start.2 = (f32[3072,128]{1,0:T(8,128)S(1)}, f32[3072,128]{1,0:T(8,128)S(1)}, u32[]{:S(2)}, u32[]{:S(2)}) collective-permute-start(f32[3072,128]{1,0:T(8,128)S(1)} %add.35), channel_id=1, source_target_pairs={{0,4},{1,5},{2,6},{3,7},{4,0},{5,1},{6,2},{7,3},{8,12},{9,13},{10,... | collective-permute-start | bytes 4718600 | tf_op jit(solution)/shard_map/ppermute | solution.py:35
  98.6 78.4 %copy-start.1 = (f32[1,96,128]{2,1,0:T(8,128)S(1)}, f32[1,96,128]{2,1,0:T(8,128)}, u32[]{:S(2)}) copy-start(f32[1,96,128]{2,1,0:T(8,128)} %param.6) | copy-start | bytes 147460
  98.6 37.4 %collective-permute-start.3 = (f32[3072,128]{1,0:T(8,128)S(1)}, f32[3072,128]{1,0:T(8,128)S(1)}, u32[]{:S(2)}, u32[]{:S(2)}) collective-permute-start(f32[3072,128]{1,0:T(8,128)S(1)} %add.36), channel_id=1, source_target_pairs={{0,8},{1,9},{2,10},{3,11},{4,12},{5,13},{6,14},{7,15},{8,0},{9,1},... | collective-permute-start | bytes 4718600 | tf_op jit(solution)/shard_map/ppermute | solution.py:35
  136.2 37.8 %collective-permute-start.4 = (f32[3072,128]{1,0:T(8,128)S(1)}, f32[3072,128]{1,0:T(8,128)S(1)}, u32[]{:S(2)}, u32[]{:S(2)}) collective-permute-start(f32[3072,128]{1,0:T(8,128)S(1)} %add.37), channel_id=1, source_target_pairs={{0,16},{1,17},{2,18},{3,19},{4,20},{5,21},{6,22},{7,23},{8,24},{9,... | collective-permute-start | bytes 4718600 | tf_op jit(solution)/shard_map/ppermute | solution.py:35
  174.0 3.0 collective-permute-start.5
  184.6 5.3 %collective-permute-start.6 = (f32[3072,128]{0,1:T(8,128)S(1)}, f32[3072,128]{0,1:T(8,128)S(1)}, u32[]{:S(2)}, u32[]{:S(2)}) collective-permute-start(f32[3072,128]{0,1:T(8,128)S(1)} %fusion), channel_id=1, source_target_pairs={{0,1},{1,0},{2,3},{3,2},{4,5},{5,4},{6,7},{7,6},{8,9},{9,8},{10,11... | collective-permute-start | bytes 4718600 | tf_op jit(solution)/shard_map/ppermute | solution.py:35
  190.1 38.3 %collective-permute-start.7 = (f32[3072,128]{0,1:T(8,128)S(1)}, f32[3072,128]{0,1:T(8,128)S(1)}, u32[]{:S(2)}, u32[]{:S(2)}) collective-permute-start(f32[3072,128]{0,1:T(8,128)S(1)} %add.40), channel_id=1, source_target_pairs={{0,2},{1,3},{2,0},{3,1},{4,6},{5,7},{6,4},{7,5},{8,10},{9,11},{10,... | collective-permute-start | bytes 4718600 | tf_op jit(solution)/shard_map/ppermute | solution.py:35
  228.6 39.0 %collective-permute-start.8 = (f32[3072,128]{0,1:T(8,128)S(1)}, f32[3072,128]{0,1:T(8,128)S(1)}, u32[]{:S(2)}, u32[]{:S(2)}) collective-permute-start(f32[3072,128]{0,1:T(8,128)S(1)} %add.41), channel_id=1, source_target_pairs={{0,4},{1,5},{2,6},{3,7},{4,0},{5,1},{6,2},{7,3},{8,12},{9,13},{10,... | collective-permute-start | bytes 4718600 | tf_op jit(solution)/shard_map/ppermute | solution.py:35
  267.8 36.6 %collective-permute-start.9 = (f32[3072,128]{0,1:T(8,128)S(1)}, f32[3072,128]{0,1:T(8,128)S(1)}, u32[]{:S(2)}, u32[]{:S(2)}) collective-permute-start(f32[3072,128]{0,1:T(8,128)S(1)} %add.42), channel_id=1, source_target_pairs={{0,8},{1,9},{2,10},{3,11},{4,12},{5,13},{6,14},{7,15},{8,0},{9,1},... | collective-permute-start | bytes 4718600 | tf_op jit(solution)/shard_map/ppermute | solution.py:35
  304.6 37.2 %collective-permute-start.10 = (f32[3072,128]{0,1:T(8,128)S(1)}, f32[3072,128]{0,1:T(8,128)S(1)}, u32[]{:S(2)}, u32[]{:S(2)}) collective-permute-start(f32[3072,128]{0,1:T(8,128)S(1)} %add.43), channel_id=1, source_target_pairs={{0,16},{1,17},{2,18},{3,19},{4,20},{5,21},{6,22},{7,23},{8,24},{9,... | collective-permute-start | bytes 4718600 | tf_op jit(solution)/shard_map/ppermute | solution.py:35
